TPU v7x, 512 devices: a whole 4x4x16 slice. The times are simulated.
512 devices in a mesh: eig: 32 (over z_lo, x, core), tok: 16 (over y, z_hi).
Axes of the slice: x: 4, y: 4, z: 16 (z_hi: 4, z_lo: 4; z = z_hi * 4 + z_lo), core: 2. Of those that a mesh axis runs over, the one named last changes fastest.
Arguments:
- query_grad: float32 [7168, 2048], P('eig', 'tok'), may hold values from -6 to 6
- basis_in: float32 [2048, 2048], P('tok', 'eig'), may hold values from -0.125 to 0.125
- basis_out: float32 [7168, 7168], P('eig', 'tok'), may hold values from -0.0625 to 0.0625
- spectrum: float32 [7168, 2048], P('tok', 'eig'), may hold values from 0.02 to 20
- activations: float32 [4096, 2048], P('tok', 'eig'), may hold values from -0.125 to 0.125
- out_grads: float32 [4096, 7168], P('tok', 'eig'), may hold values from -0.0625 to 0.0625
Outputs:
- influence: float32 [4096], P('tok')
All inputs are finite; a program needn't handle non-finite values.
Results may differ from a plain program's by a relative error of at most 0.000094.
Values sent between devices are 32-bit elements; how exact they have to be, the bound alone decides.
A program may use at most 64 MiB of HBM per device.

v0:
```python
import jax
import jax.numpy as jnp
from jax import lax
from jax.sharding import PartitionSpec as P

damping = 0.1


def contract_first(left, right):
    return lax.dot_general(
        left,
        right,
        (((0,), (0,)), ((), ())),
        precision=lax.Precision.HIGHEST,
        preferred_element_type=jnp.float32,
    )


def contract_last(left, right):
    return lax.dot_general(
        left,
        right,
        (((1,), (1,)), ((), ())),
        precision=lax.Precision.HIGHEST,
        preferred_element_type=jnp.float32,
    )


def plain_dot(left, right):
    return jnp.dot(left, right, precision=lax.Precision.HIGHEST, preferred_element_type=jnp.float32)


def body(query_grad, basis_in, basis_out, spectrum, activations, out_grads):
    input_rows = lax.all_gather(basis_in, "eig", axis=1, tiled=True)
    rotated_in = lax.psum(plain_dot(query_grad, input_rows), "tok")
    rotated_whole = contract_first(basis_out, rotated_in)
    rotated_part = lax.psum_scatter(rotated_whole, "eig", scatter_dimension=1, tiled=True)
    scaled_part = rotated_part / (spectrum + damping)
    scaled = lax.all_gather(scaled_part, "eig", axis=1, tiled=True)
    back_out = lax.psum(plain_dot(basis_out, scaled), "tok")
    full_acts = lax.all_gather(activations, "eig", axis=1, tiled=True)
    precond = contract_last(back_out, input_rows)
    mapped = contract_last(full_acts, lax.all_gather(precond, "tok", axis=1, tiled=True))
    token_terms = jnp.sum(mapped * out_grads, axis=1)
    return lax.psum(token_terms, "eig")


def solution(mesh):
    in_specs = (
        P("eig", "tok"),
        P("tok", "eig"),
        P("eig", "tok"),
        P("tok", "eig"),
        P("tok", "eig"),
        P("tok", "eig"),
    )
    out_specs = P("tok")
    return jax.shard_map(body, mesh=mesh, in_specs=in_specs, out_specs=out_specs, check_vma=False)
```

profile of v0, /device:TPU:1, one launch (start us, length us, event | category | flops | bytes accessed | tf_op | source)
XLA Modules:
  0.0 1091.7 jit_solution(6881868478980649362)
XLA Ops:
  6.5 0.0 copy-start
  6.5 0.0 all-gather.5.cloned.1.call-start
  6.5 0.7 all-gather.5.cloned.1.call-update
  7.3 0.0 all-reduce.3.cloned.1.call-start
  7.3 71.9 %all-gather.5.cloned.1.call-done = f32[128,2048]{0,1:T(8,128)} async-done(((f32[128,64]{0,1:T(8,128)}), f32[128,2048]{0,1:T(8,128)}) %all-gather.5.cloned.1.call-update) | async-done | bytes 1048592 | tf_op jit(solution)/shard_map/all_gather | solution.py:34
  79.2 4.2 fusion.2
  83.4 0.0 all-reduce.3.cloned.1.call-update
  83.4 0.0 reduce-scatter.2.cloned.1.call-start
  83.5 247.2 %all-reduce.3.cloned.1.call-done = f32[224,2048]{1,0:T(8,128)} async-done(((f32[224,2048]{1,0:T(8,128)}), f32[224,2048]{1,0:T(8,128)}) %all-reduce.3.cloned.1.call-update) | async-done | bytes 1835024 | tf_op jit(solution)/shard_map/psum | solution.py:35
  330.7 9.8 convolution_bitcast_fusion
  340.5 0.0 reduce-scatter.2.cloned.1.call-update
  340.6 0.0 all-gather.7.cloned.1.call-start
  340.6 156.1 %reduce-scatter.2.cloned.1.call-done = f32[448,64]{0,1:T(8,128)} async-done(((f32[448,2048]{0,1:T(8,128)}), f32[448,64]{0,1:T(8,128)}) %reduce-scatter.2.cloned.1.call-update) | async-done | bytes 114704 | tf_op jit(solution)/shard_map/reduce_scatter | solution.py:37
  496.7 0.0 copy-done.3
  496.7 1.6 add_divide_fusion
  498.3 0.0 all-gather.7.cloned.1.call-update
  498.3 0.0 all-reduce.5.cloned.1.call-start
  498.4 69.9 %all-gather.7.cloned.1.call-done = f32[448,2048]{0,1:T(8,128)} async-done(((f32[448,64]{0,1:T(8,128)}), f32[448,2048]{0,1:T(8,128)}) %all-gather.7.cloned.1.call-update) | async-done | bytes 3670032 | tf_op jit(solution)/shard_map/all_gather | solution.py:39
  568.3 7.0 convolution_bitcast_fusion.1
  575.3 0.0 all-reduce.5.cloned.1.call-update
  575.3 0.0 copy-start.2
  575.3 0.0 all-gather.11.cloned.1.call-start
  575.4 0.5 all-gather.11.cloned.1.call-update
  575.9 0.2 all-gather.9.cloned.1.call-start
  576.2 264.0 %all-reduce.5.cloned.1.call-done = f32[224,2048]{0,1:T(8,128)} async-done(((f32[224,2048]{0,1:T(8,128)}), f32[224,2048]{0,1:T(8,128)}) %all-reduce.5.cloned.1.call-update) | async-done | bytes 1835024 | tf_op jit(solution)/shard_map/psum | solution.py:40
  840.1 5.6 fusion.3
  845.8 0.0 all-gather.9.cloned.1.call-update
  845.8 68.6 %all-gather.11.cloned.1.call-done = f32[256,2048]{0,1:T(8,128)} async-done(((f32[256,64]{0,1:T(8,128)}), f32[256,2048]{0,1:T(8,128)}) %all-gather.11.cloned.1.call-update) | async-done | bytes 2097168 | tf_op jit(solution)/shard_map/all_gather | solution.py:41
  914.4 96.7 %all-gather.9.cloned.1.call-done = f32[224,2048]{1,0:T(8,128)} async-done(((f32[224,128]{1,0:T(8,128)}), f32[224,2048]{1,0:T(8,128)}) %all-gather.9.cloned.1.call-update) | async-done | bytes 1835024 | tf_op jit(solution)/shard_map/all_gather | solution.py:43
  1011.1 0.0 copy-done.2
  1011.1 3.8 fusion.1
  1014.9 69.9 %psum.23 = f32[256]{0:T(256)} all-reduce(f32[256]{0:T(256)S(1)} %fusion.1), channel_id=1, replica_groups=mesh['eig'=32,'tok'=16] {'eig'}, use_global_device_ids=true, to_apply=%region_4.0 | all-reduce | flops 256 | bytes 2048 | tf_op jit(solution)/shard_map/psum | solution.py:45
  (4 shorter events, 0.0 us)
Async XLA Ops:
  6.5 324.2 %copy-start = (f32[224,448]{1,0:T(8,128)S(1)}, f32[224,448]{1,0:T(8,128)}, u32[]{:S(2)}) copy-start(f32[224,448]{1,0:T(8,128)} %param.8) | copy-start | bytes 1204228
  6.5 72.7 %all-gather.5.cloned.1.call-start = ((), (), s32[]{:S(2)}) async-start(), calls=%async_computation.1 | async-start | bytes 1081344 | tf_op jit(solution)/shard_map/all_gather | solution.py:34
  7.3 323.4 %all-reduce.3.cloned.1.call-start = ((), (), s32[]{:S(2)}) async-start(), calls=%async_computation.2 | async-start | bytes 3670016 | tf_op jit(solution)/shard_map/psum | solution.py:35
  83.4 413.3 %reduce-scatter.2.cloned.1.call-start = ((), (), s32[]{:S(2)}) async-start(), calls=%async_computation.3 | async-start | bytes 4325376 | tf_op jit(solution)/shard_map/reduce_scatter | solution.py:37
  340.5 156.2 %copy-start.3 = (f32[448,64]{0,1:T(8,128)S(1)}, f32[448,64]{0,1:T(8,128)}, u32[]{:S(2)}) copy-start(f32[448,64]{0,1:T(8,128)} %param.9) | copy-start | bytes 344068
  340.6 227.7 %all-gather.7.cloned.1.call-start = ((), (), s32[]{:S(2)}) async-start(), calls=%async_computation.4 | async-start | bytes 4325376 | tf_op jit(solution)/shard_map/all_gather | solution.py:39
  498.3 341.8 %all-reduce.5.cloned.1.call-start = ((), (), s32[]{:S(2)}) async-start(), calls=%async_computation.5 | async-start | bytes 4194304 | tf_op jit(solution)/shard_map/psum | solution.py:40
  575.3 264.8 %copy-start.1 = (f32[128,2048]{0,1:T(8,128)S(1)}, f32[128,2048]{0,1:T(8,128)}, u32[]{:S(2)}) copy-start(f32[128,2048]{0,1:T(8,128)} %all-gather.5.cloned.1.call-done) | copy-start | bytes 3145732
  575.3 435.8 %copy-start.2 = (f32[256,224]{0,1:T(8,128)S(1)}, f32[256,224]{0,1:T(8,128)}, u32[]{:S(2)}) copy-start(f32[256,224]{0,1:T(8,128)} %param.11) | copy-start | bytes 688132
  575.3 339.0 %all-gather.11.cloned.1.call-start = ((), (), s32[]{:S(2)}) async-start(), calls=%async_computation.7 | async-start | bytes 2162688 | tf_op jit(solution)/shard_map/all_gather | solution.py:41
  575.9 435.2 %all-gather.9.cloned.1.call-start = ((), (), s32[]{:S(2)}) async-start(), calls=%async_computation.6 | async-start | bytes 1949696 | tf_op jit(solution)/shard_map/all_gather | solution.py:43
Sparse Core Ops, SparseCore 0:
  9.5 69.6 all-gather.4
  83.5 247.1 all-reduce.2
  340.7 155.9 reduce-scatter.1
  498.9 69.3 all-gather.6
  575.5 264.6 all-reduce.4
  842.3 71.9 all-gather.10
  917.8 93.2 all-gather.8
where the time goes:
time: 1090 us
  waiting for transfers between devices  976 us (90%)
  blocking collectives  69.9 us (6%)
  matrix products  30.4 us (3%)
  between operations  13.5 us (1%)
    psum x1, waiting for transfers between devices, body(): back_out = lax.psum(plain_dot(basis_out, scaled), 'tok')  264 us
    psum x1, waiting for transfers between devices, body(): rotated_in = lax.psum(plain_dot(query_grad, input_rows), 'tok')  247 us
    reduce_scatter x1, waiting for transfers between devices, body(): lax.psum_scatter(rotated_whole, 'eig', scatter_dimension=1, tiled=True)  156 us
    all_gather x1, waiting for transfers between devices, body(): lax.all_gather(precond, 'tok', axis=1, tiled=True)  96.7 us
    all_gather x1, waiting for transfers between devices, body(): input_rows = lax.all_gather(basis_in, 'eig', axis=1, tiled=True)  71.9 us
    all_gather x1, waiting for transfers between devices, body(): scaled = lax.all_gather(scaled_part, 'eig', axis=1, tiled=True)  69.9 us
    psum x1, blocking collectives, body(): return lax.psum(token_terms, 'eig')  69.9 us
    all_gather x1, waiting for transfers between devices, body(): full_acts = lax.all_gather(activations, 'eig', axis=1, tiled=True)  68.6 us
  transfers between devices with their start and end apart: 7, of which 7 were waited for; matrix products, arithmetic and copies ran while one was open for 1% of the time, Pallas kernels for 0%

commit v1 on v0

v1 whole, which is shorter than its diff:
```python
import jax
import jax.numpy as jnp
from jax import lax
from jax.experimental import pallas as pl
from jax.experimental.pallas import tpu as pltpu
from jax.sharding import PartitionSpec as P

damping = 0.1
MESH = pl.DeviceIdType.MESH
F32, BF16 = jnp.float32, jnp.bfloat16
SIZE = dict(zl=4, x=4, k=2, y=4, zh=4)
N_SEMS = 128


def coords():
    e, t = lax.axis_index("eig"), lax.axis_index("tok")
    return dict(zl=e // 8, x=(e // 2) % 4, k=e % 2, y=t // 4, zh=t % 4)


def place(c, **other):
    d = dict(c, **other)
    return (d["zl"] * 8 + d["x"] * 2 + d["k"], d["y"] * 4 + d["zh"])


def peer(c, axis, d):
    return place(c, **{axis: lax.rem(c[axis] + d, SIZE[axis])})


def at_distance(c, axis, d):
    return lax.rem(c[axis] + d, SIZE[axis])


def split(v):
    hi = v.astype(BF16)
    return hi, (v - hi.astype(F32)).astype(BF16)


def mm(left, right, dims=((1,), (0,))):
    return lax.dot_general(left, right, (dims, ((), ())), preferred_element_type=F32)


def dot3(lh, ll, cat, dims=((1,), (0,))):
    n = cat.shape[1] // 2
    wide = mm(lh, cat, dims)
    return wide[:, :n] + wide[:, n:] + mm(ll, cat[:, :n], dims)


def both(v):
    return jnp.concatenate(split(v), axis=1)


def kernel(
    g, b, o, sp, a, og, out,
    oA, oB, ohi, olo, gall, asw, bsw, spsw, ball, aA, aB, wall, ogA, ogB,
    tp, tk, ts, tz, tA, tB, sall, scat, bp, bz, f0, f1, f2, f3, f4, f5, f6,
    ss, rs, ls,
):
    c = coords()
    x, y, zl, zh, k = c["x"], c["y"], c["zl"], c["zh"], c["k"]
    used = [0]
    sent = []

    def remote(src, dst, device):
        i = used[0]
        used[0] += 1
        return pltpu.make_async_remote_copy(
            src_ref=src, dst_ref=dst, send_sem=ss.at[i], recv_sem=rs.at[i], device_id=device, device_id_type=MESH
        )

    def start(copies):
        for q in copies:
            q.start()
            sent.append(q)
        return copies

    def arrived(copies):
        for q in copies:
            q.wait_recv()

    class Maybe:
        def __init__(self, own, src, dst, device):
            self.own, self.far = own, remote(src, dst, device)
            self.near = pltpu.make_async_copy(src, dst, ls.at[used[0]])

        def start(self):
            pl.when(jnp.logical_not(self.own))(self.far.start)
            pl.when(self.own)(self.near.start)

        def wait_recv(self):
            pl.when(jnp.logical_not(self.own))(self.far.wait_recv)
            pl.when(self.own)(self.near.wait)

        def wait_send(self):
            pl.when(jnp.logical_not(self.own))(self.far.wait_send)

    swap_yz = dict(y=zl, zl=y)
    swap_xz = place(c, x=zh, zh=x)
    own_yz, own_xz = y == zl, x == zh

    barrier = pltpu.get_barrier_semaphore()
    for axis in ("x", "y", "zl", "zh", "k"):
        for d in range(1, SIZE[axis]):
            pl.semaphore_signal(barrier, inc=1, device_id=peer(c, axis, d), device_id_type=MESH)

    @pl.when(jnp.logical_not(own_yz))
    def _():
        pl.semaphore_signal(barrier, inc=1, device_id=place(c, **swap_yz), device_id_type=MESH)
        pl.semaphore_signal(barrier, inc=1, device_id=place(c, k=1 - k, **swap_yz), device_id_type=MESH)

    @pl.when(jnp.logical_not(own_xz))
    def _():
        pl.semaphore_signal(barrier, inc=1, device_id=swap_xz, device_id_type=MESH)

    own = [
        pltpu.make_async_copy(o.at[pl.ds(0, 112)], oA.at[y, x], ls.at[0]),
        pltpu.make_async_copy(o.at[pl.ds(112, 112)], oB.at[x, y], ls.at[1]),
    ]
    used[0] = 2
    for q in own:
        q.start()
    pl.semaphore_wait(barrier, 16 - jnp.where(own_yz, 2, 0) - jnp.where(own_xz, 1, 0))

    def gather_first(bufA, bufB, srcA=None, srcB=None):
        srcA = bufA.at[y, x] if srcA is None else srcA
        srcB = bufB.at[x, y] if srcB is None else srcB
        la = [remote(srcA, bufA.at[y, x], peer(c, "x", d)) for d in (1, 3, 2)]
        lb = [remote(srcB, bufB.at[x, y], peer(c, "y", d)) for d in (1, 3, 2)]
        return start(la), start(lb)

    def gather_second(bufA, bufB, first):
        arrived(first[0])
        la = start([remote(bufA.at[y], bufA.at[y], peer(c, "y", d)) for d in (1, 3, 2)])
        arrived(first[1])
        lb = start([remote(bufB.at[x], bufB.at[x], peer(c, "x", d)) for d in (1, 3, 2)])
        return la + lb

    qg = start([Maybe(own_xz, g, gall.at[x], swap_xz)])
    o1 = gather_first(oA, oB, o.at[pl.ds(0, 112)], o.at[pl.ds(112, 112)])
    qb, qa, qs = [], [], []
    for list_, src, dst, rows in ((qb, b, bsw, 64), (qa, a, asw, 128), (qs, sp, spsw, 224)):
        list_.append(Maybe(own_yz, src.at[pl.ds(pl.multiple_of(k * rows, rows), rows)], dst.at[k], place(c, **swap_yz)))
        list_.append(
            remote(src.at[pl.ds(pl.multiple_of((1 - k) * rows, rows), rows)], dst.at[k], place(c, k=1 - k, **swap_yz))
        )
        start(list_)
    qog = start([
        Maybe(own_xz, og.at[pl.ds(0, 128)], ogA.at[y, zh], swap_xz),
        Maybe(own_xz, og.at[pl.ds(128, 128)], ogB.at[zh, y], swap_xz),
    ])

    arrived(qg)
    g2 = start([remote(gall.at[zh], gall.at[zh], peer(c, "zh", d)) for d in (1, 3, 2)])

    arrived(qb)
    ball[zl, zh, k] = jnp.concatenate([bsw[0], bsw[1]], axis=1)
    b2 = start([remote(ball.at[zl, zh, k], ball.at[zl, zh, k], peer(c, "zh", d)) for d in (1, 3, 2)])

    for q in own:
        q.wait()
    o2 = gather_second(oA, oB, o1)

    arrived(qa)
    av = jnp.concatenate([asw[0], asw[1]], axis=1)
    aA[y, x] = av[:64]
    aB[x, y] = av[64:]
    a1 = gather_first(aA, aB)

    arrived(b2)
    b3 = start([remote(ball.at[zl, :, k], ball.at[zl, :, k], peer(c, "zl", d)) for d in (1, 3, 2)])
    a2 = gather_second(aA, aB, a1)
    arrived(b3)
    b4 = start([remote(ball.at[:, :, k], ball.at[:, :, k], peer(c, "k", 1))])

    arrived(g2)
    gcat = both(gall[...].reshape(896, 128))
    arrived(o2)

    def t_step(i, _):
        for j in range(4):
            for half, block in ((0, oA[i, j]), (1, oB[j, i])):
                hi, lo = split(block)
                ohi[i, j, half * 112 : half * 112 + 112] = hi
                olo[i, j, half * 112 : half * 112 + 112] = lo
        part = dot3(ohi[i].reshape(896, 448), olo[i].reshape(896, 448), gcat, ((0,), (0,)))
        tp[0, i] = part[:224]
        tp[1, i] = part[224:]
        return 0

    lax.fori_loop(0, 4, t_step, 0)
    t1 = start([remote(tp.at[1 - k], tk, peer(c, "k", 1))])

    arrived(a2)
    arrived(b4)
    bcat = both(ball[...].reshape(2048, 128))
    blocks = [(i, j) for i in range(4) for j in range(4)]
    arows = jnp.concatenate(
        [
            jnp.concatenate([aA[i, j] for i, j in blocks], axis=1),
            jnp.concatenate([aB[j, i] for i, j in blocks], axis=1),
        ],
        axis=0,
    )
    wall[zl, zh, k] = dot3(*split(arows), bcat)

    arrived(t1)
    ts[...] = tp[k] + tk[...]
    t2 = start([remote(ts.at[at_distance(c, "zl", d)], tz.at[d], peer(c, "zl", d)) for d in (1, 3, 2)])
    w1 = start([remote(wall.at[zl, zh, k], wall.at[zl, zh, k], peer(c, "zh", d)) for d in (1, 3, 2)])
    arrived(t2)
    tv = ts[zl] + tz[1] + tz[2] + tz[3]
    tA[y, x] = tv[:112]
    tB[x, y] = tv[112:]
    t3 = gather_first(tA, tB)
    t4 = gather_second(tA, tB, t3)
    arrived(qog)
    og1 = gather_first(ogA, ogB)
    arrived(w1)
    w2 = start([remote(wall.at[zl, :, k], wall.at[zl, :, k], peer(c, "zl", d)) for d in (1, 3, 2)])
    arrived(qs)
    spv = jnp.concatenate([spsw[0], spsw[1]], axis=1) + damping
    arrived(t4)

    trows = jnp.concatenate(
        [
            jnp.concatenate([tA[i, j] for i, j in blocks], axis=1),
            jnp.concatenate([tB[j, i] for i, j in blocks], axis=1),
        ],
        axis=0,
    )
    bcat = both(ball[...].reshape(2048, 128))
    sall[zl, k] = dot3(*split(trows), bcat) / spv
    s1 = start([remote(sall.at[zl, k], sall.at[zl, k], peer(c, "zl", d)) for d in (1, 3, 2)])
    s2 = start([remote(sall.at[zl, k], sall.at[zl, k], peer(c, "k", 1))])
    for q, d in zip(s1, (1, 3, 2)):
        q.wait_recv()
        origin = lax.rem(zl - d + 4, 4)
        s2 += start([remote(sall.at[origin, k], sall.at[origin, k], peer(c, "k", 1))])
    og2 = gather_second(ogA, ogB, og1)
    arrived(w2)
    w3 = start([remote(wall.at[:, :, k], wall.at[:, :, k], peer(c, "k", 1))])
    arrived(s2)

    scat[...] = both(sall[...].reshape(1792, 128)).reshape(4, 448, 256)

    def b_step(j, _):
        total = dot3(ohi[0, j], olo[0, j], scat[0])
        for i in range(1, 4):
            total = total + dot3(ohi[i, j], olo[i, j], scat[i])
        bp[j] = total
        return 0

    lax.fori_loop(0, 4, b_step, 0)
    k1 = start([remote(bp.at[at_distance(c, "zh", d)], bz.at[d], peer(c, "zh", d)) for d in (1, 3, 2)])
    arrived(og2)
    arrived(w3)
    arrived(k1)
    kcat = both(bp[zh] + bz[1] + bz[2] + bz[3])

    def f_step(n, _):
        i, j = n // 4, n % 4
        rows = jnp.concatenate([ogA[i, j], ogB[j, i]], axis=0)
        v = dot3(*split(rows), kcat) * wall[i, j].reshape(256, 128)
        f0[i, j] = jnp.sum(v.T.reshape(16, 8, 256), axis=0)
        return 0

    lax.fori_loop(0, 16, f_step, 0)
    arrived(start([remote(f0.at[at_distance(c, "y", d)], f1.at[d], peer(c, "y", d)) for d in (1, 3, 2)]))
    f2[...] = f0[y] + f1[1] + f1[2] + f1[3]
    arrived(start([remote(f2.at[at_distance(c, "zh", d)], f3.at[d], peer(c, "zh", d)) for d in (1, 3, 2)]))
    f4[x] = f2[zh] + f3[1] + f3[2] + f3[3]
    arrived(start([remote(f4.at[x], f4.at[x], peer(c, "x", d)) for d in (1, 3, 2)]))
    f5[zl] = f4[0] + f4[1] + f4[2] + f4[3]
    arrived(start([remote(f5.at[zl], f5.at[zl], peer(c, "zl", d)) for d in (1, 3, 2)]))
    f6[k] = f5[0] + f5[1] + f5[2] + f5[3]
    arrived(start([remote(f6.at[k], f6.at[k], peer(c, "k", 1))]))
    out[...] = jnp.sum(f6[0] + f6[1], axis=0, keepdims=True)
    for q in sent:
        q.wait_send()


def body(query_grad, basis_in, basis_out, spectrum, activations, out_grads):
    def vmem(*shape, dtype=F32):
        return pltpu.VMEM(shape, dtype)

    out = pl.pallas_call(
        kernel,
        out_shape=jax.ShapeDtypeStruct((1, 256), F32),
        in_specs=[pl.BlockSpec(memory_space=pl.ANY)] * 6,
        out_specs=pl.BlockSpec(memory_space=pltpu.VMEM),
        scratch_shapes=[
            vmem(4, 4, 112, 448),
            vmem(4, 4, 112, 448),
            vmem(4, 4, 224, 448, dtype=BF16),
            vmem(4, 4, 224, 448, dtype=BF16),
            vmem(4, 224, 128),
            vmem(2, 128, 64),
            vmem(2, 64, 64),
            vmem(2, 224, 64),
            vmem(4, 4, 2, 64, 128),
            vmem(4, 4, 64, 128),
            vmem(4, 4, 64, 128),
            vmem(4, 4, 2, 128, 128),
            vmem(4, 4, 128, 224),
            vmem(4, 4, 128, 224),
            vmem(2, 4, 224, 128),
            vmem(4, 224, 128),
            vmem(4, 224, 128),
            vmem(4, 224, 128),
            vmem(4, 4, 112, 128),
            vmem(4, 4, 112, 128),
            vmem(4, 2, 224, 128),
            vmem(4, 448, 256, dtype=BF16),
            vmem(4, 224, 128),
            vmem(4, 224, 128),
            vmem(4, 4, 8, 256),
            vmem(4, 4, 8, 256),
            vmem(4, 8, 256),
            vmem(4, 8, 256),
            vmem(4, 8, 256),
            vmem(4, 8, 256),
            vmem(2, 8, 256),
            pltpu.SemaphoreType.DMA((N_SEMS,)),
            pltpu.SemaphoreType.DMA((N_SEMS,)),
            pltpu.SemaphoreType.DMA((N_SEMS,)),
        ],
        compiler_params=pltpu.CompilerParams(
            collective_id=0, has_side_effects=True, vmem_limit_bytes=56 * 1024 * 1024
        ),
    )(query_grad, basis_in, basis_out, spectrum, activations, out_grads)
    return out.reshape(256)


def solution(mesh):
    in_specs = (
        P("eig", "tok"),
        P("tok", "eig"),
        P("eig", "tok"),
        P("tok", "eig"),
        P("tok", "eig"),
        P("tok", "eig"),
    )
    out_specs = P("tok")
    return jax.shard_map(body, mesh=mesh, in_specs=in_specs, out_specs=out_specs, check_vma=False)
```

time: 1090 us -> 257 us (0.24)
  waiting for transfers between devices: 976 us -> 0 us
  Pallas kernels: 0 us -> 252 us
  blocking collectives: 69.9 us -> 0 us
  matrix products: 30.4 us -> 0 us
  between operations: 13.5 us -> 0.02 us
    psum x2 -> x0, waiting for transfers between devices: 511 us -> none  [the longest x1 264 us: body(): back_out = lax.psum(plain_dot(basis_out, scaled), 'tok')]
    all_gather x4 -> x0, waiting for transfers between devices: 307 us -> none  [the longest x1 96.7 us: body(): lax.all_gather(precond, 'tok', axis=1, tiled=True)]
    pallas_call x0 -> x1, Pallas kernels: none -> 252 us  [body(): pl.pallas_call(kernel, out_shape=jax.ShapeDtypeStruct((1, 256), F32), in_...]
    reduce_scatter x1 -> x0, waiting for transfers between devices: 156 us -> none  [body(): lax.psum_scatter(rotated_whole, 'eig', scatter_dimension=1, tiled=True)]
    psum x1 -> x0, blocking collectives: 69.9 us -> none  [body(): return lax.psum(token_terms, 'eig')]
    dot_general x5 -> x0, matrix products: 30.4 us -> none  [the longest x2 11.2 us: plain_dot(): jnp.dot(left, right, precision=lax.Precision.HIGHEST, preferred_element_t...]
  transfers between devices with their start and end apart: 7 -> 0, of which waited for: 7 -> 0; matrix products, arithmetic and copies ran while one was open for 1% -> 0% of each run, Pallas kernels for 0% -> 0%
where the time goes in v1:
time: 257 us
  Pallas kernels  252 us (98%)
  local copies, waits for them, and re-layouts  5.13 us (2%)
    pallas_call x1, Pallas kernels, body(): pl.pallas_call(kernel, out_shape=jax.ShapeDtypeStruct((1, 256), F32), in_...  252 us

profile of v1, /device:TPU:1, one launch (start us, length us, event | category | flops | bytes accessed | tf_op | source)
XLA Modules:
  0.0 257.2 jit_solution(5612747720384284355)
XLA Ops:
  0.0 0.0 copy-start.2
  0.0 0.0 copy-start.1
  0.0 1.5 copy.7.b
  1.5 0.0 copy-done.2
  1.5 0.0 copy-start
  1.5 0.8 copy.9.a
  2.3 0.0 copy-done.1
  2.3 0.8 copy.8.sp
  3.1 0.0 copy-done
  3.1 0.8 copy.10.og
  3.9 252.0 %shard_map.64 = f32[1,256]{1,0:T(1,128)} custom-call(f32[224,128]{1,0:T(8,128)} %g.1, f32[128,64]{1,0:T(8,128)} %copy.7.b, f32[224,448]{1,0:T(8,128)} %o.1, f32[448,64]{1,0:T(8,128)} %copy.8.sp, f32[256,64]{1,0:T(8,128)} %copy.9.a, f32[256,224]{1,0:T(8,128)} %copy.10.og), custom_call_target="tpu_custom_call" | custom-call | tf_op jit(solution)/shard_map/pallas_call | solution.py:285
  256.0 0.0 copy-start.3
  256.0 0.7 copy-done.3
  256.6 0.6 copy.12
Async XLA Ops:
  0.0 1.5 copy-start.2
  0.0 2.3 copy-start.1
  1.5 1.6 copy-start
  256.0 0.7 copy-start.3

commit v2 on v1

v2 whole, which is shorter than its diff:
```python
import jax
import jax.numpy as jnp
from jax import lax
from jax.experimental import pallas as pl
from jax.experimental.pallas import tpu as pltpu
from jax.sharding import PartitionSpec as P

damping = 0.1
MESH = pl.DeviceIdType.MESH
F32, BF16 = jnp.float32, jnp.bfloat16
SIZE = dict(zl=4, x=4, k=2, y=4, zh=4)
N_SEMS = 256
ORDER = (1, 3, 2)


def coords():
    e, t = lax.axis_index("eig"), lax.axis_index("tok")
    return dict(zl=e // 8, x=(e // 2) % 4, k=e % 2, y=t // 4, zh=t % 4)


def place(c, **other):
    d = dict(c, **other)
    return (d["zl"] * 8 + d["x"] * 2 + d["k"], d["y"] * 4 + d["zh"])


def peer(c, axis, d):
    return place(c, **{axis: lax.rem(c[axis] + d, SIZE[axis])})


def at_distance(c, axis, d):
    return lax.rem(c[axis] + d, SIZE[axis])


def split(v):
    hi = v.astype(BF16)
    return hi, (v - hi.astype(F32)).astype(BF16)


def mm(left, right, dims=((1,), (0,))):
    return lax.dot_general(left, right, (dims, ((), ())), preferred_element_type=F32)


def dot3(lh, ll, cat, dims=((1,), (0,))):
    n = cat.shape[1] // 2
    wide = mm(lh, cat, dims)
    return wide[:, :n] + wide[:, n:] + mm(ll, cat[:, :n], dims)


def both(v, axis):
    return jnp.concatenate(split(v), axis=axis)


def kernel(
    g, bt, o, spt, at, ogt, out,
    oA, oB, ohi, olo, gz, gall, spsw, damped, ball, bcat, aAB, wall, wcat, ogAB,
    tp, tk, ts, tz, tA, tB, sall, scat, bp, bz, f0, f1, f2, f3, f4, f5,
    ss, rs, ls,
):
    c = coords()
    x, y, zl, zh, k = c["x"], c["y"], c["zl"], c["zh"], c["k"]
    used = [0]
    sent = []

    def remote(src, dst, device):
        i = used[0]
        used[0] += 1
        return pltpu.make_async_remote_copy(
            src_ref=src, dst_ref=dst, send_sem=ss.at[i], recv_sem=rs.at[i], device_id=device, device_id_type=MESH
        )

    def start(copies):
        for q in copies:
            q.start()
            sent.append(q)
        return copies

    def arrived(copies):
        for q in copies:
            q.wait_recv()

    class Maybe:
        def __init__(self, own, src, dst, device):
            self.own, self.far = own, remote(src, dst, device)
            self.near = pltpu.make_async_copy(src, dst, ls.at[used[0]])

        def start(self):
            pl.when(jnp.logical_not(self.own))(self.far.start)
            pl.when(self.own)(self.near.start)

        def wait_recv(self):
            pl.when(jnp.logical_not(self.own))(self.far.wait_recv)
            pl.when(self.own)(self.near.wait)

        def wait_send(self):
            pl.when(jnp.logical_not(self.own))(self.far.wait_send)

    def to_peers(axis, src, dst):
        return start([remote(src, dst, peer(c, axis, d)) for d in ORDER])

    def scatter(axis, src, dst):
        return start([remote(src.at[at_distance(c, axis, d)], dst.at[d], peer(c, axis, d)) for d in ORDER])

    def summed(own, got):
        return own + got[1] + got[2] + got[3]

    swap_yz = place(c, y=zl, zl=y)
    swap_yz_far = place(c, y=zl, zl=y, k=1 - k)
    own_yz = y == zl
    plane = [
        place(c, x=at_distance(c, "x", i), y=at_distance(c, "y", j)) for i in range(4) for j in range(4) if i or j
    ]
    column = [
        place(c, zl=at_distance(c, "zl", i), zh=at_distance(c, "zh", j)) for i in range(4) for j in range(4) if i or j
    ]
    z = zh * 4 + zl

    def along_z(d):
        other = lax.rem(z + d, 16)
        return place(c, zl=other % 4, zh=other // 4)

    og_half = zh // 2
    og_slot = ogAB.at[og_half, y + og_half * (x - y), x + og_half * (y - x), zh % 2]

    own = [
        pltpu.make_async_copy(o.at[pl.ds(0, 112)], oA.at[y, x], ls.at[0]),
        pltpu.make_async_copy(o.at[pl.ds(112, 112)], oB.at[x, y], ls.at[1]),
        pltpu.make_async_copy(g, gz.at[zh], ls.at[2]),
        pltpu.make_async_copy(ogt.at[pl.ds(pl.multiple_of(zh * 56, 8), 56)], og_slot, ls.at[3]),
    ]
    used[0] = 4
    for q in own:
        q.start()

    barrier = pltpu.get_barrier_semaphore()
    for partner in plane + column + [peer(c, "k", 1)]:
        pl.semaphore_signal(barrier, inc=1, device_id=partner, device_id_type=MESH)

    @pl.when(jnp.logical_not(own_yz))
    def _():
        pl.semaphore_signal(barrier, inc=1, device_id=swap_yz, device_id_type=MESH)
        pl.semaphore_signal(barrier, inc=1, device_id=swap_yz_far, device_id_type=MESH)

    pl.semaphore_wait(barrier, 33 - jnp.where(own_yz, 2, 0))

    def gather_first(bufA, bufB, srcA=None, srcB=None):
        srcA = bufA.at[y, x] if srcA is None else srcA
        srcB = bufB.at[x, y] if srcB is None else srcB
        return to_peers("x", srcA, bufA.at[y, x]), to_peers("y", srcB, bufB.at[x, y])

    def gather_second(bufA, bufB, first):
        arrived(first[0])
        second = to_peers("y", bufA.at[y], bufA.at[y])
        arrived(first[1])
        return second + to_peers("x", bufB.at[x], bufB.at[x])

    class Pipeline:
        def __init__(self, buf, src, one, two):
            self.buf, self.src, self.one, self.two, self.sends = buf, src, one, two, {}

        def slot(self, d2, d1, rows=None):
            ref = self.buf.at[at_distance(c, self.two, d2), at_distance(c, self.one, d1)]
            return ref if rows is None else ref.at[pl.ds(*rows)]

        def go(self, key, src, dst, axis, d):
            self.sends[key] = start([remote(src, dst, peer(c, axis, d))])

        def spread(self, e):
            src = self.src if e == 0 else self.slot(0, e)
            for d in (1, 3):
                self.go(("spread", e, d), src, self.slot(0, e), self.two, d)

        def begin(self):
            for d in (1, 3):
                self.go(("own", d), self.src, self.slot(0, 0), self.one, d)
            self.spread(0)

        def relay(self):
            arrived(self.sends["own", 1] + self.sends["own", 3])
            for d, rows in ((1, (0, 56)), (3, (56, 56))):
                ref = self.slot(0, 4 - d, rows)
                self.go(("relay", d), ref, ref, self.one, d)
            self.spread(3)
            self.spread(1)

        def opposite(self):
            arrived(self.sends["relay", 1] + self.sends["relay", 3])
            self.spread(2)

        def forward(self, e):
            arrived(self.sends["spread", e, 1] + self.sends["spread", e, 3])
            for d, rows in ((1, (0, 56)), (3, (56, 56))):
                if e in (0, 2) or e == 4 - d:
                    ref = self.slot(4 - d, e, rows if e in (0, 2) else None)
                    self.go(("forward", e, d), ref, ref, self.two, d)

        def end(self):
            for key, q in self.sends.items():
                if key[0] == "forward":
                    arrived(q)

    class Ring:
        def __init__(self, buf):
            self.buf, self.step, self.last = buf, 0, None

        def advance(self, steps=1):
            for _ in range(steps):
                if self.last is not None:
                    arrived(self.last)
                s = self.step
                self.step += 1
                self.last = []
                for d in (1, -1):
                    if s < (8 if d == 1 else 7):
                        block = lax.rem(z - d * s + 16, 16)
                        ref = self.buf.at[block % 4, block // 4, k]
                        self.last += start([remote(ref, ref, along_z(d + 16))])

        def end(self):
            self.advance(8 - self.step)
            arrived(self.last)
            return start([remote(self.buf.at[:, :, k], self.buf.at[:, :, k], peer(c, "k", 1))])

    g1 = to_peers("zh", g, gz.at[zh])
    qb = start([Maybe(own_yz, bt, ball.at[y, zh, k], swap_yz)])
    oa = Pipeline(oA, o.at[pl.ds(0, 112)], "x", "y")
    ob = Pipeline(oB, o.at[pl.ds(112, 112)], "y", "x")
    oa.begin()
    ob.begin()
    a_slot = aAB.at[k, zl + k * (x - zl), x + k * (zl - x)]
    tokens_near = at.at[:, pl.ds(pl.multiple_of(k * 128, 128), 128)]
    tokens_far = at.at[:, pl.ds(pl.multiple_of((1 - k) * 128, 128), 128)]
    qa = start([Maybe(own_yz, tokens_near, a_slot, swap_yz), remote(tokens_far, a_slot, swap_yz_far)])
    for p in (oa, ob):
        p.relay()
    bring = Ring(ball)
    arrived(qb)
    bring.advance(1)
    for p in (oa, ob):
        p.forward(0)
    for q in own:
        q.wait()
    bring.advance(1)
    for p in (oa, ob):
        p.opposite()
    arrived(g1)
    g2 = start([remote(gz.at[at_distance(c, "x", d)], gall.at[x], peer(c, "x", d)) for d in ORDER])
    gall[x] = gz[x]
    qs = start([Maybe(own_yz, spt, spsw.at[k], swap_yz)])
    qog = start([
        remote(ogt.at[pl.ds(pl.multiple_of(at_distance(c, "zh", d) * 56, 8), 56)], og_slot, peer(c, "zh", d))
        for d in ORDER
    ])
    bring.advance(1)
    for p in (oa, ob):
        p.forward(3)
        p.forward(1)
    bring.advance(2)
    for p in (oa, ob):
        p.forward(2)
    arrived(qa)
    a1 = gather_first(aAB.at[0], aAB.at[1])
    bring.advance(1)

    arrived(g2)
    gcat = both(gall[...].reshape(896, 128), 1)
    for p in (oa, ob):
        p.end()

    def t_step(i, _):
        for j in range(4):
            for half, block in ((0, oA[i, j]), (1, oB[j, i])):
                hi, lo = split(block)
                ohi[i, j, half * 112 : half * 112 + 112] = hi
                olo[i, j, half * 112 : half * 112 + 112] = lo
        part = dot3(ohi[i].reshape(896, 448), olo[i].reshape(896, 448), gcat, ((0,), (0,)))
        tp[0, i] = part[:224]
        tp[1, i] = part[224:]
        return 0

    lax.fori_loop(0, 4, t_step, 0)
    t1 = start([remote(tp.at[1 - k], tk, peer(c, "k", 1))])
    a2 = gather_second(aAB.at[0], aAB.at[1], a1)
    arrived(t1)
    ts[...] = tp[k] + tk[...]
    t2 = scatter("zl", ts, tz)
    b4 = bring.end()
    arrived(b4)
    blocks = [(i, j) for i in range(4) for j in range(4)]
    btv = jnp.concatenate([ball[i, j].reshape(128, 128) for i, j in blocks], axis=1)
    bcat[...] = both(btv, 0)
    arrived(t2)
    tv = summed(ts[zl], tz)
    tA[y, x] = tv[:112]
    tB[x, y] = tv[112:]
    t3 = gather_first(tA, tB)
    t4 = gather_second(tA, tB, t3)

    arrived(a2)
    arows = jnp.concatenate([aAB[0, i, j] if h == 0 else aAB[1, j, i] for i, j in blocks for h in range(2)], axis=0)
    wall[zl, zh, k] = dot3(bcat[:128], bcat[128:], both(arows, 1))
    wring = Ring(wall)
    wring.advance(1)
    arrived(qs)
    arrived(start([remote(spsw.at[k], spsw.at[k], peer(c, "k", 1))]))
    sp_rows = jnp.concatenate([spsw[0], spsw[1]], axis=0).T + damping
    damped[0] = sp_rows[:224]
    damped[1] = sp_rows[224:]
    wring.advance(1)
    arrived(qog)
    og1 = gather_first(ogAB.at[0], ogAB.at[1])
    arrived(t4)

    trows = jnp.concatenate(
        [
            jnp.concatenate([tA[i, j] for i, j in blocks], axis=1),
            jnp.concatenate([tB[j, i] for i, j in blocks], axis=1),
        ],
        axis=0,
    )
    thi, tlo = split(trows)
    wide = mm(thi, bcat[...], ((1,), (1,)))
    rotated = wide[:, :128] + wide[:, 128:] + mm(tlo, bcat[:128], ((1,), (1,)))
    sall[zl, k] = rotated / damped[k]
    s1 = to_peers("zl", sall.at[zl, k], sall.at[zl, k])
    s2 = start([remote(sall.at[zl, k], sall.at[zl, k], peer(c, "k", 1))])
    for q, d in zip(s1, ORDER):
        arrived([q])
        origin = lax.rem(zl - d + 4, 4)
        s2 += start([remote(sall.at[origin, k], sall.at[origin, k], peer(c, "k", 1))])
    wring.advance(1)
    og2 = gather_second(ogAB.at[0], ogAB.at[1], og1)
    wring.advance(1)
    arrived(s2)

    scat[...] = both(sall[...].reshape(1792, 128), 1).reshape(4, 448, 256)

    def b_step(j, _):
        total = dot3(ohi[0, j], olo[0, j], scat[0])
        for i in range(1, 4):
            total = total + dot3(ohi[i, j], olo[i, j], scat[i])
        for q in range(4):
            bp[q, j] = total[q * 56 : q * 56 + 56]
        return 0

    lax.fori_loop(0, 4, b_step, 0)
    k1 = scatter("zh", bp, bz)
    w3 = wring.end()
    arrived(w3)

    def w_step(n, _):
        i, j = n // 4, n % 4
        hi, lo = split(jnp.concatenate([wall[i, j, 0], wall[i, j, 1]], axis=1))
        wcat[n, :128] = hi
        wcat[n, 128:256] = lo
        wcat[n, 256:] = hi
        return 0

    lax.fori_loop(0, 16, w_step, 0)
    arrived(og2)
    arrived(k1)
    khi, klo = split(summed(bp[zh], bz).reshape(224, 128))
    kcat = jnp.concatenate([khi, khi, klo], axis=1)

    def f_step(n, _):
        i, j = n // 4, n % 4
        m = mm(kcat, wcat[n])
        half = j // 2
        v = jnp.zeros((56, 256), F32)
        for n_x in range(4):
            v = v + m[n_x * 56 : n_x * 56 + 56] * ogAB[half, i + half * (n_x - i), n_x + half * (i - n_x), j % 2]
        f0[i, j] = jnp.sum(v.reshape(7, 8, 256), axis=0)
        return 0

    lax.fori_loop(0, 16, f_step, 0)
    row = lax.broadcasted_iota(jnp.int32, (8, 256), 0)
    for i in range(4):
        line = jnp.zeros((8, 256), F32)
        for j in range(4):
            line = jnp.where(row == j, jnp.sum(f0[i, j], axis=0, keepdims=True), line)
        f1[i] = line
    got = []
    for n, partner in enumerate(plane):
        i, j = (n + 1) // 4, (n + 1) % 4
        got += start([remote(f1.at[at_distance(c, "y", j)], f2.at[x, y], partner)])
    f2[x, y] = f1[y]
    arrived(got)
    total = jnp.sum(f2[...].reshape(16, 8, 256), axis=0)
    for j in range(4):
        f3[j] = jnp.broadcast_to(total[j : j + 1], (8, 256))
    got = []
    for n, partner in enumerate(column):
        i, j = (n + 1) // 4, (n + 1) % 4
        got += start([remote(f3.at[at_distance(c, "zh", j)], f4.at[k, zl, zh], partner)])
    f4[k, zl, zh] = f3[zh]
    arrived(got)
    f5[k] = jnp.sum(f4[k].reshape(16, 8, 256), axis=0)
    arrived(start([remote(f5.at[k], f5.at[k], peer(c, "k", 1))]))
    out[...] = (f5[0] + f5[1])[:1]
    for q in sent:
        q.wait_send()


def body(query_grad, basis_in, basis_out, spectrum, activations, out_grads):
    def vmem(*shape, dtype=F32):
        return pltpu.VMEM(shape, dtype)

    out = pl.pallas_call(
        kernel,
        out_shape=jax.ShapeDtypeStruct((1, 256), F32),
        in_specs=[pl.BlockSpec(memory_space=pl.ANY)] * 6,
        out_specs=pl.BlockSpec(memory_space=pltpu.VMEM),
        scratch_shapes=[
            vmem(4, 4, 112, 448),
            vmem(4, 4, 112, 448),
            vmem(4, 4, 224, 448, dtype=BF16),
            vmem(4, 4, 224, 448, dtype=BF16),
            vmem(4, 224, 128),
            vmem(4, 224, 128),
            vmem(2, 64, 448),
            vmem(2, 224, 128),
            vmem(4, 4, 2, 64, 128),
            vmem(256, 2048, dtype=BF16),
            vmem(2, 4, 4, 64, 128),
            vmem(4, 4, 2, 128, 128),
            vmem(16, 384, 256, dtype=BF16),
            vmem(2, 4, 4, 2, 56, 256),
            vmem(2, 4, 224, 128),
            vmem(4, 224, 128),
            vmem(4, 224, 128),
            vmem(4, 224, 128),
            vmem(4, 4, 112, 128),
            vmem(4, 4, 112, 128),
            vmem(4, 2, 224, 128),
            vmem(4, 448, 256, dtype=BF16),
            vmem(4, 4, 56, 128),
            vmem(4, 4, 56, 128),
            vmem(4, 4, 8, 256),
            vmem(4, 8, 256),
            vmem(4, 4, 8, 256),
            vmem(4, 8, 256),
            vmem(2, 4, 4, 8, 256),
            vmem(2, 8, 256),
            pltpu.SemaphoreType.DMA((N_SEMS,)),
            pltpu.SemaphoreType.DMA((N_SEMS,)),
            pltpu.SemaphoreType.DMA((N_SEMS,)),
        ],
        compiler_params=pltpu.CompilerParams(
            collective_id=0, has_side_effects=True, vmem_limit_bytes=56 * 1024 * 1024
        ),
    )(query_grad, basis_in.T, basis_out, spectrum.T, activations.T, out_grads.T)
    return out.reshape(256)


def solution(mesh):
    in_specs = (
        P("eig", "tok"),
        P("tok", "eig"),
        P("eig", "tok"),
        P("tok", "eig"),
        P("tok", "eig"),
        P("tok", "eig"),
    )
    out_specs = P("tok")
    return jax.shard_map(body, mesh=mesh, in_specs=in_specs, out_specs=out_specs, check_vma=False)
```

time: 257 us -> 191 us (0.74)
  Pallas kernels: 252 us -> 190 us
  local copies, waits for them, and re-layouts: 5.13 us -> 1.22 us
    pallas_call x1, Pallas kernels: 252 us -> 190 us  [body(): pl.pallas_call(kernel, out_shape=jax.ShapeDtypeStruct((1, 256), F32), in_...]
    unnamed x13 -> x3, local copies, waits for them, and re-layouts: 5.13 us -> 1.22 us
where the time goes in v2:
time: 191 us
  Pallas kernels  190 us (99%)
    pallas_call x1, Pallas kernels, body(): pl.pallas_call(kernel, out_shape=jax.ShapeDtypeStruct((1, 256), F32), in_...  190 us

profile of v2, /device:TPU:1, one launch (start us, length us, event | category | flops | bytes accessed | tf_op | source)
XLA Modules:
  0.0 191.3 jit_solution(13001801688597004496)
XLA Ops:
  0.0 190.1 %shard_map.64 = f32[1,256]{1,0:T(1,128)} custom-call(f32[224,128]{1,0:T(8,128)} %g.1, f32[64,128]{1,0:T(8,128)} %bitcast.8, f32[224,448]{1,0:T(8,128)} %o.1, f32[64,448]{1,0:T(8,128)} %bitcast.6, f32[64,256]{1,0:T(8,128)} %bitcast.7, f32[224,256]{1,0:T(8,128)} %bitcast.5), custom_call_target="tpu_custom_call" | custom-call | tf_op jit(solution)/shard_map/pallas_call | solution.py:407
  190.1 0.0 copy-start
  190.1 0.7 copy-done
  190.8 0.6 copy.8
Async XLA Ops:
  190.1 0.7 copy-start

commit v3 on v2

--- a/solution.py
+++ b/solution.py
@@ -232,46 +232,60 @@
     qa = start([Maybe(own_yz, tokens_near, a_slot, swap_yz), remote(tokens_far, a_slot, swap_yz_far)])
     for p in (oa, ob):
         p.relay()
-    bring = Ring(ball)
-    arrived(qb)
-    bring.advance(1)
     for p in (oa, ob):
         p.forward(0)
     for q in own:
         q.wait()
-    bring.advance(1)
     for p in (oa, ob):
         p.opposite()
     arrived(g1)
     g2 = start([remote(gz.at[at_distance(c, "x", d)], gall.at[x], peer(c, "x", d)) for d in ORDER])
     gall[x] = gz[x]
+    bring = Ring(ball)
+    arrived(qb)
+    bring.advance(1)
+    for p in (oa, ob):
+        p.forward(3)
+        p.forward(1)
+    bring.advance(2)
+    arrived(qa)
+    a1 = gather_first(aAB.at[0], aAB.at[1])
+    for p in (oa, ob):
+        p.forward(2)
+    bring.advance(1)
     qs = start([Maybe(own_yz, spt, spsw.at[k], swap_yz)])
     qog = start([
         remote(ogt.at[pl.ds(pl.multiple_of(at_distance(c, "zh", d) * 56, 8), 56)], og_slot, peer(c, "zh", d))
         for d in ORDER
     ])
-    bring.advance(1)
-    for p in (oa, ob):
-        p.forward(3)
-        p.forward(1)
-    bring.advance(2)
-    for p in (oa, ob):
-        p.forward(2)
-    arrived(qa)
-    a1 = gather_first(aAB.at[0], aAB.at[1])
+    a2 = gather_second(aAB.at[0], aAB.at[1], a1)
+
+    def convert(half, i, j):
+        hi, lo = split(oA[i, j] if half == 0 else oB[j, i])
+        ohi[i, j, half * 112 : half * 112 + 112] = hi
+        olo[i, j, half * 112 : half * 112 + 112] = lo
+
+    def early(n, _):
+        for d in (0, 1, 3):
+            convert(0, at_distance(c, "y", d), n)
+            convert(1, n, at_distance(c, "x", d))
+        return 0
+
+    def late(n, _):
+        convert(0, at_distance(c, "y", 2), n)
+        convert(1, n, at_distance(c, "x", 2))
+        return 0
+
+    lax.fori_loop(0, 4, early, 0)
     bring.advance(1)
 
     arrived(g2)
     gcat = both(gall[...].reshape(896, 128), 1)
     for p in (oa, ob):
         p.end()
+    lax.fori_loop(0, 4, late, 0)
 
     def t_step(i, _):
-        for j in range(4):
-            for half, block in ((0, oA[i, j]), (1, oB[j, i])):
-                hi, lo = split(block)
-                ohi[i, j, half * 112 : half * 112 + 112] = hi
-                olo[i, j, half * 112 : half * 112 + 112] = lo
         part = dot3(ohi[i].reshape(896, 448), olo[i].reshape(896, 448), gcat, ((0,), (0,)))
         tp[0, i] = part[:224]
         tp[1, i] = part[224:]
@@ -279,27 +293,28 @@
 
     lax.fori_loop(0, 4, t_step, 0)
     t1 = start([remote(tp.at[1 - k], tk, peer(c, "k", 1))])
-    a2 = gather_second(aAB.at[0], aAB.at[1], a1)
+    bring.advance(1)
     arrived(t1)
     ts[...] = tp[k] + tk[...]
     t2 = scatter("zl", ts, tz)
-    b4 = bring.end()
-    arrived(b4)
+    arrived(bring.end())
     blocks = [(i, j) for i in range(4) for j in range(4)]
     btv = jnp.concatenate([ball[i, j].reshape(128, 128) for i, j in blocks], axis=1)
     bcat[...] = both(btv, 0)
+
+    arrived(a2)
+    arows = jnp.concatenate([aAB[0, i, j] if h == 0 else aAB[1, j, i] for i, j in blocks for h in range(2)], axis=0)
+    wall[zl, zh, k] = dot3(bcat[:128], bcat[128:], both(arows, 1))
+    wring = Ring(wall)
+    wring.advance(1)
     arrived(t2)
     tv = summed(ts[zl], tz)
     tA[y, x] = tv[:112]
     tB[x, y] = tv[112:]
     t3 = gather_first(tA, tB)
+    wring.advance(1)
     t4 = gather_second(tA, tB, t3)
-
-    arrived(a2)
-    arows = jnp.concatenate([aAB[0, i, j] if h == 0 else aAB[1, j, i] for i, j in blocks for h in range(2)], axis=0)
-    wall[zl, zh, k] = dot3(bcat[:128], bcat[128:], both(arows, 1))
-    wring = Ring(wall)
-    wring.advance(1)
+    wring.advance(2)
     arrived(qs)
     arrived(start([remote(spsw.at[k], spsw.at[k], peer(c, "k", 1))]))
     sp_rows = jnp.concatenate([spsw[0], spsw[1]], axis=0).T + damping
@@ -323,13 +338,12 @@
     sall[zl, k] = rotated / damped[k]
     s1 = to_peers("zl", sall.at[zl, k], sall.at[zl, k])
     s2 = start([remote(sall.at[zl, k], sall.at[zl, k], peer(c, "k", 1))])
+    wring.advance(1)
+    og2 = gather_second(ogAB.at[0], ogAB.at[1], og1)
     for q, d in zip(s1, ORDER):
         arrived([q])
         origin = lax.rem(zl - d + 4, 4)
         s2 += start([remote(sall.at[origin, k], sall.at[origin, k], peer(c, "k", 1))])
-    wring.advance(1)
-    og2 = gather_second(ogAB.at[0], ogAB.at[1], og1)
-    wring.advance(1)
     arrived(s2)
 
     scat[...] = both(sall[...].reshape(1792, 128), 1).reshape(4, 448, 256)
@@ -386,16 +400,16 @@
     arrived(got)
     total = jnp.sum(f2[...].reshape(16, 8, 256), axis=0)
     for j in range(4):
-        f3[j] = jnp.broadcast_to(total[j : j + 1], (8, 256))
+        f3[j] = total[j : j + 1]
     got = []
     for n, partner in enumerate(column):
         i, j = (n + 1) // 4, (n + 1) % 4
         got += start([remote(f3.at[at_distance(c, "zh", j)], f4.at[k, zl, zh], partner)])
     f4[k, zl, zh] = f3[zh]
     arrived(got)
-    f5[k] = jnp.sum(f4[k].reshape(16, 8, 256), axis=0)
+    f5[k] = jnp.sum(f4[k].reshape(16, 1, 256), axis=0)
     arrived(start([remote(f5.at[k], f5.at[k], peer(c, "k", 1))]))
-    out[...] = (f5[0] + f5[1])[:1]
+    out[...] = f5[0] + f5[1]
     for q in sent:
         q.wait_send()
 
@@ -437,9 +451,9 @@
             vmem(4, 4, 8, 256),
             vmem(4, 8, 256),
             vmem(4, 4, 8, 256),
-            vmem(4, 8, 256),
-            vmem(2, 4, 4, 8, 256),
-            vmem(2, 8, 256),
+            vmem(4, 1, 256),
+            vmem(2, 4, 4, 1, 256),
+            vmem(2, 1, 256),
             pltpu.SemaphoreType.DMA((N_SEMS,)),
             pltpu.SemaphoreType.DMA((N_SEMS,)),
             pltpu.SemaphoreType.DMA((N_SEMS,)),

time: 191 us -> 178 us (0.932)
  Pallas kernels: 190 us -> 176 us
    pallas_call x1, Pallas kernels: 190 us -> 176 us  [body(): pl.pallas_call(kernel, out_shape=jax.ShapeDtypeStruct((1, 256), F32), in_...]
where the time goes in v3:
time: 178 us
  Pallas kernels  176 us (99%)
    pallas_call x1, Pallas kernels, body(): pl.pallas_call(kernel, out_shape=jax.ShapeDtypeStruct((1, 256), F32), in_...  176 us

profile of v3, /device:TPU:1, one launch (start us, length us, event | category | flops | bytes accessed | tf_op | source)
XLA Modules:
  0.0 177.6 jit_solution(18444544069009799055)
XLA Ops:
  0.0 176.3 %shard_map.64 = f32[1,256]{1,0:T(1,128)} custom-call(f32[224,128]{1,0:T(8,128)} %g.1, f32[64,128]{1,0:T(8,128)} %bitcast.8, f32[224,448]{1,0:T(8,128)} %o.1, f32[64,448]{1,0:T(8,128)} %bitcast.6, f32[64,256]{1,0:T(8,128)} %bitcast.7, f32[224,256]{1,0:T(8,128)} %bitcast.5), custom_call_target="tpu_custom_call" | custom-call | tf_op jit(solution)/shard_map/pallas_call | solution.py:421
  176.3 0.0 copy-start
  176.4 0.7 copy-done
  177.0 0.6 copy.8
Async XLA Ops:
  176.3 0.7 copy-start

commit v4 on v3

--- a/solution.py
+++ b/solution.py
@@ -338,8 +338,8 @@
     sall[zl, k] = rotated / damped[k]
     s1 = to_peers("zl", sall.at[zl, k], sall.at[zl, k])
     s2 = start([remote(sall.at[zl, k], sall.at[zl, k], peer(c, "k", 1))])
-    wring.advance(1)
     og2 = gather_second(ogAB.at[0], ogAB.at[1], og1)
+    wring.advance(2)
     for q, d in zip(s1, ORDER):
         arrived([q])
         origin = lax.rem(zl - d + 4, 4)

time: 178 us -> 177 us (level)
  no operation moved by 1% of the time
where the time goes in v4:
time: 177 us; the launch traced here: 176 us
  Pallas kernels  175 us (99%)
    pallas_call x1, Pallas kernels, body(): pl.pallas_call(kernel, out_shape=jax.ShapeDtypeStruct((1, 256), F32), in_...  175 us

profile of v4, /device:TPU:1, one launch (start us, length us, event | category | flops | bytes accessed | tf_op | source)
XLA Modules:
  0.0 176.4 jit_solution(18263966685593072305)
XLA Ops:
  0.0 175.2 %shard_map.64 = f32[1,256]{1,0:T(1,128)} custom-call(f32[224,128]{1,0:T(8,128)} %g.1, f32[64,128]{1,0:T(8,128)} %bitcast.8, f32[224,448]{1,0:T(8,128)} %o.1, f32[64,448]{1,0:T(8,128)} %bitcast.6, f32[64,256]{1,0:T(8,128)} %bitcast.7, f32[224,256]{1,0:T(8,128)} %bitcast.5), custom_call_target="tpu_custom_call" | custom-call | tf_op jit(solution)/shard_map/pallas_call | solution.py:421
  175.2 0.0 copy-start
  175.2 0.7 copy-done
  175.9 0.6 copy.8
Async XLA Ops:
  175.2 0.7 copy-start
